TPU v7x, 32 devices: a whole 2x2x4 slice. The times are simulated.
32 devices in a mesh: dp: 2 (over x), row: 4 (over z), col: 4 (over y, core).
Axes of the slice: x: 2, y: 2, z: 4, core: 2. Of those that a mesh axis runs over, the one named last changes fastest.
Arguments:
- layer_input: float32 [2, 1024, 256], P('dp', 'col', 'row'), may hold values from -6 to 6
- segment_ids: int32 [2, 1024], P('dp'), may hold values from 0 to 2, as said below
- head_projection_weights: float32 [2, 3, 256, 256], P(None, None, 'row', 'col'), may hold values from -0.375 to 0.375
- output_projection_weights: float32 [2, 256, 256], P(None, 'col', 'row'), may hold values from -1.5 to 1.5
- up_projection_weights: float32 [2, 256, 1024], P(None, 'row', 'col'), may hold values from -0.375 to 0.375
- down_projection_weights: float32 [2, 1024, 256], P(None, 'col', 'row'), may hold values from -0.1875 to 0.1875
- head_moment: float32 [2, 3, 256, 256], P(None, None, 'row', 'col'), may hold values from -6 to 6
- out_moment: float32 [2, 256, 256], P(None, 'col', 'row'), may hold values from -28 to 28
- up_moment: float32 [2, 256, 1024], P(None, 'row', 'col'), may hold values from -64 to 64
- down_moment: float32 [2, 1024, 256], P(None, 'col', 'row'), may hold values from -128 to 128
- norm_params: float32 [2, 4, 256], P(None, None, 'row')
- norm_first: float32 [2, 4, 256], P(None, None, 'row'), may hold values from -28 to 28
- norm_second: float32 [2, 4, 256], P(None, None, 'row'), may hold values from 2.048 to 8.192
- output_grad: float32 [2, 1024, 256], P('dp', 'col', 'row'), may hold values from -6 to 6
Outputs:
- layer_output: float32 [2, 1024, 256], P('dp', 'col', 'row')
- input_grad: float32 [2, 1024, 256], P('dp', 'col', 'row')
- head_updated: float32 [2, 3, 256, 256], P(None, None, 'row', 'col')
- out_updated: float32 [2, 256, 256], P(None, 'col', 'row')
- up_updated: float32 [2, 256, 1024], P(None, 'row', 'col')
- down_updated: float32 [2, 1024, 256], P(None, 'col', 'row')
- head_momentum: float32 [2, 3, 256, 256], P(None, None, 'row', 'col')
- out_momentum: float32 [2, 256, 256], P(None, 'col', 'row')
- up_momentum: float32 [2, 256, 1024], P(None, 'row', 'col')
- down_momentum: float32 [2, 1024, 256], P(None, 'col', 'row')
- first_moment: float32 [2, 4, 256], P(None, None, 'row')
- second_moment: float32 [2, 4, 256], P(None, None, 'row')
- norm_updated: float32 [2, 4, 256], P(None, None, 'row')
Inputs may be any that keep to these rules, and one draw needn't show every extreme that they name: `segment_ids`: along each sequence the ids never fall, and each of 0, 1 and 2 occurs in every sequence.
All inputs are finite; a program needn't handle non-finite values.
Results may differ from a plain program's by a relative error of at most 0.0003.
Values sent between devices are 32-bit elements; how exact they have to be, the bound alone decides.
No kernel may reach another device: no remote copies, remote signals or barrier semaphores. Data moves between devices by JAX's collectives and lax.ppermute only.
A program may use at most 128 MiB of HBM per device.

v0:
```python
import math

import jax
import jax.numpy as jnp
from jax import lax
from jax.sharding import PartitionSpec as P

D = 256
FF = 1024
LEN = 1024
LAYERS = 2
NS_STEPS = 5
STEP = 10
HD = 64


highest_precision = lax.Precision.HIGHEST
norm_eps = 1e-05
newton_coefs = (3.4445, -4.775, 2.0315)
frob_eps = 1e-07
muon_decay = 0.95
muon_rate = 0.5
adam_first = 0.9
adam_second = 0.999
adam_eps = 1e-08
adam_rate = 0.2
masked_score = -1e30


def from_root(x, axis, root):
    mine = lax.axis_index(axis) == root
    return lax.psum(jnp.where(mine, x, jnp.zeros_like(x)), axis)


def gather_cols(values):
    return lax.all_gather(values, "col", axis=1, tiled=True)


def gather_rows(values):
    return lax.all_gather(values, "row", axis=1, tiled=True)


def scatter_rows(values):
    return lax.psum_scatter(values, "row", scatter_dimension=1, tiled=True)


def scatter_cols(values):
    return lax.psum_scatter(values, "col", scatter_dimension=1, tiled=True)


def feature_totals(values):
    return lax.psum(values, "row")


def share_block(block, owner):
    return from_root(block, "dp", owner)


def normalize(values, gain, shift):
    mean_value = feature_totals(jnp.sum(values, axis=-1)) / D
    center = values - mean_value[..., None]
    variance = feature_totals(jnp.sum(center * center, axis=-1)) / D
    inverse = lax.rsqrt(variance + norm_eps)[..., None]
    normed = center * inverse
    return (normed * gain + shift, normed, inverse)


def normalize_back(grad_out, normed, inverse, gain):
    scaled = grad_out * gain
    first_sum, second_sum = feature_totals(
        (jnp.sum(scaled, axis=-1), jnp.sum(scaled * normed, axis=-1))
    )
    grad_in = inverse * (scaled - first_sum[..., None] / D - normed * (second_sum[..., None] / D))
    return (grad_in, jnp.sum(grad_out * normed, axis=(0, 1)), jnp.sum(grad_out, axis=(0, 1)))


def gelu_value(values):
    return jax.nn.gelu(values, approximate=False)


def gelu_slope(values):
    return (
        0.5 * (1.0 + lax.erf(values * 0.7071067811865476))
        + values * jnp.exp(-0.5 * values * values) * 0.3989422804014327
    )


def split_heads(values):
    return values.reshape(values.shape[0], values.shape[1], values.shape[2] // HD, HD)


def masked_scores(queries, key_rows, query_ids, key_ids):
    scores = jnp.einsum(
        "sqhd,skhd->shqk", split_heads(queries), split_heads(key_rows), precision=highest_precision
    ) * HD ** (-0.5)
    allowed = query_ids[:, None, :, None] == key_ids[:, None, None, :]
    return jnp.where(allowed, scores, masked_score)


def attend_forward(queries, key_rows, value_rows, query_ids, key_ids):
    scores = masked_scores(queries, key_rows, query_ids, key_ids)
    maximum = jnp.max(scores, axis=-1, keepdims=True)
    raised = jnp.exp(scores - maximum)
    totals = jnp.sum(raised, axis=-1, keepdims=True)
    shares = raised / totals
    attended = jnp.einsum(
        "shqk,skhd->sqhd", shares, split_heads(value_rows), precision=highest_precision
    )
    return (attended.reshape(queries.shape), maximum + jnp.log(totals))


def attend_backward(
    queries, key_rows, value_rows, query_ids, key_ids, attended, log_total, grad_attended
):
    scores = masked_scores(queries, key_rows, query_ids, key_ids)
    shares = jnp.exp(scores - log_total)
    grad_split = split_heads(grad_attended)
    grad_shares = jnp.einsum(
        "sqhd,skhd->shqk", grad_split, split_heads(value_rows), precision=highest_precision
    )
    row_inner = jnp.transpose(jnp.sum(grad_split * split_heads(attended), axis=-1), (0, 2, 1))[
        ..., None
    ]
    grad_scores = shares * (grad_shares - row_inner) * HD ** (-0.5)
    grad_queries = jnp.einsum(
        "shqk,skhd->sqhd", grad_scores, split_heads(key_rows), precision=highest_precision
    ).reshape(queries.shape)
    grad_keys = jnp.einsum(
        "shqk,sqhd->skhd", grad_scores, split_heads(queries), precision=highest_precision
    ).reshape(key_rows.shape)
    grad_values = jnp.einsum(
        "shqk,sqhd->skhd", shares, grad_split, precision=highest_precision
    ).reshape(value_rows.shape)
    return (grad_queries, jnp.concatenate([grad_keys, grad_values], axis=-1))


def orthogonal(matrix):
    height, breadth = matrix.shape
    current = matrix.T if height > breadth else matrix
    current = current / (jnp.sqrt(jnp.sum(current * current)) + frob_eps)
    for repeat in range(NS_STEPS):
        gram_matrix = jnp.dot(current, current.T, precision=highest_precision)
        polynomial = newton_coefs[1] * gram_matrix + newton_coefs[2] * jnp.dot(
            gram_matrix, gram_matrix, precision=highest_precision
        )
        current = newton_coefs[0] * current + jnp.dot(
            polynomial, current, precision=highest_precision
        )
    current = current.T if height > breadth else current
    return current * math.sqrt(max(height, breadth))


def on_device(
    layer_input,
    segment_ids,
    head_projection_weights,
    output_projection_weights,
    up_projection_weights,
    down_projection_weights,
    head_moment,
    out_moment,
    up_moment,
    down_moment,
    norm_params,
    norm_first,
    norm_second,
    output_grad,
):
    row_index = lax.axis_index("row")
    col_index = lax.axis_index("col")
    dp_index = lax.axis_index("dp")
    dp_count = lax.axis_size("dp")
    row_count = lax.axis_size("row")
    col_count = lax.axis_size("col")
    query_span = LEN // row_count
    query_ids = lax.dynamic_slice_in_dim(segment_ids, row_index * query_span, query_span, 1)
    head_width = head_projection_weights.shape[-1]
    feature_span = head_projection_weights.shape[2]
    hidden_span = up_projection_weights.shape[-1]
    seq_count = layer_input.shape[0]
    hidden = layer_input
    kept = []
    for current_layer_index in range(LAYERS):
        gathered_input_rows = gather_cols(hidden)
        partial_heads = jnp.einsum(
            "uex,bxk->uebk",
            gathered_input_rows,
            head_projection_weights[current_layer_index],
            precision=highest_precision,
        )
        local_heads = scatter_rows(partial_heads.reshape(seq_count, LEN, 3 * head_width))
        queries = local_heads[..., :head_width]
        key_value = gather_rows(local_heads[..., head_width:])
        key_rows = key_value[..., :head_width]
        value_rows = key_value[..., head_width:]
        attended, log_total = attend_forward(queries, key_rows, value_rows, query_ids, segment_ids)
        attended_stack = gather_rows(attended)
        branch = scatter_cols(
            jnp.einsum(
                "two,or->twr",
                attended_stack,
                output_projection_weights[current_layer_index],
                precision=highest_precision,
            )
        )
        middle, normed_first, inverse_first = normalize(
            hidden + branch,
            norm_params[current_layer_index, 0],
            norm_params[current_layer_index, 1],
        )
        gathered_middle_rows = gather_cols(middle)
        before = scatter_rows(
            jnp.einsum(
                "vzb,br->vzr",
                gathered_middle_rows,
                up_projection_weights[current_layer_index],
                precision=highest_precision,
            )
        )
        activated_stack = gather_rows(gelu_value(before))
        feed = scatter_cols(
            jnp.einsum(
                "vqe,eh->vqh",
                activated_stack,
                down_projection_weights[current_layer_index],
                precision=highest_precision,
            )
        )
        hidden, normed_second, inverse_second = normalize(
            middle + feed, norm_params[current_layer_index, 2], norm_params[current_layer_index, 3]
        )
        kept.append(
            (
                gathered_input_rows,
                queries,
                key_rows,
                value_rows,
                attended,
                log_total,
                attended_stack,
                normed_first,
                inverse_first,
                gathered_middle_rows,
                before,
                activated_stack,
                normed_second,
                inverse_second,
            )
        )
    head_grads = [None] * LAYERS
    out_grads = [None] * LAYERS
    up_grads = [None] * LAYERS
    down_grads = [None] * LAYERS
    norm_grads = [None] * LAYERS
    grad_hidden = output_grad
    for current_layer_index in reversed(range(LAYERS)):
        (
            gathered_input_rows,
            queries,
            key_rows,
            value_rows,
            attended,
            log_total,
            attended_stack,
            normed_first,
            inverse_first,
            gathered_middle_rows,
            before,
            activated_stack,
            normed_second,
            inverse_second,
        ) = kept[current_layer_index]
        grad_second, gain_two, shift_two = normalize_back(
            grad_hidden, normed_second, inverse_second, norm_params[current_layer_index, 2]
        )
        gradient_feed_stack = gather_cols(grad_second)
        down_grads[current_layer_index] = jnp.einsum(
            "pvc,pvq->cq", activated_stack, gradient_feed_stack, precision=highest_precision
        )
        grad_activated = scatter_rows(
            jnp.einsum(
                "gyn,kn->gyk",
                gradient_feed_stack,
                down_projection_weights[current_layer_index],
                precision=highest_precision,
            )
        )
        gradient_before_stack = gather_rows(grad_activated * gelu_slope(before))
        up_grads[current_layer_index] = jnp.einsum(
            "ctm,cto->mo", gathered_middle_rows, gradient_before_stack, precision=highest_precision
        )
        grad_middle = grad_second + scatter_cols(
            jnp.einsum(
                "gqz,hz->gqh",
                gradient_before_stack,
                up_projection_weights[current_layer_index],
                precision=highest_precision,
            )
        )
        grad_first, gain_one, shift_one = normalize_back(
            grad_middle, normed_first, inverse_first, norm_params[current_layer_index, 0]
        )
        gradient_branch_stack = gather_cols(grad_first)
        out_grads[current_layer_index] = jnp.einsum(
            "tvp,tvn->pn", attended_stack, gradient_branch_stack, precision=highest_precision
        )
        grad_attended = scatter_rows(
            jnp.einsum(
                "jbe,ie->jbi",
                gradient_branch_stack,
                output_projection_weights[current_layer_index],
                precision=highest_precision,
            )
        )
        grad_queries, grad_key_value = attend_backward(
            queries,
            key_rows,
            value_rows,
            query_ids,
            segment_ids,
            attended,
            log_total,
            grad_attended,
        )
        head_gradients = gather_rows(
            jnp.concatenate([grad_queries, scatter_rows(grad_key_value)], axis=-1)
        )
        head_gradients = head_gradients.reshape(seq_count, LEN, 3, head_width)
        head_grads[current_layer_index] = jnp.einsum(
            "gev,geqb->qvb", gathered_input_rows, head_gradients, precision=highest_precision
        )
        grad_hidden = grad_first + scatter_cols(
            jnp.einsum(
                "eacf,cof->eao",
                head_gradients,
                head_projection_weights[current_layer_index],
                precision=highest_precision,
            )
        )
        norm_grads[current_layer_index] = jnp.stack([gain_one, shift_one, gain_two, shift_two])
    head_sum, out_sum, up_sum, down_sum = lax.psum(
        (jnp.stack(head_grads), jnp.stack(out_grads), jnp.stack(up_grads), jnp.stack(down_grads)),
        "dp",
    )
    norm_sum = lax.psum(jnp.stack(norm_grads), ("dp", "col"))
    head_momentum = muon_decay * head_moment + head_sum
    out_momentum = muon_decay * out_moment + out_sum
    up_momentum = muon_decay * up_moment + up_sum
    down_momentum = muon_decay * down_moment + down_sum
    head_whole, out_whole, up_whole, down_whole = (
        lax.all_gather(head_momentum[None], ("row", "col"), axis=0, tiled=True),
        lax.all_gather(out_momentum[None], ("row", "col"), axis=0, tiled=True),
        lax.all_gather(up_momentum[None], ("row", "col"), axis=0, tiled=True),
        lax.all_gather(down_momentum[None], ("row", "col"), axis=0, tiled=True),
    )
    head_whole = (
        head_whole.reshape((row_count, col_count) + head_momentum.shape)
        .transpose(2, 3, 0, 4, 1, 5)
        .reshape(LAYERS, 3, D, D)
    )
    out_whole = (
        out_whole.reshape((row_count, col_count) + out_momentum.shape)
        .transpose(2, 1, 3, 0, 4)
        .reshape(LAYERS, D, D)
    )
    up_whole = (
        up_whole.reshape((row_count, col_count) + up_momentum.shape)
        .transpose(2, 0, 3, 1, 4)
        .reshape(LAYERS, D, FF)
    )
    down_whole = (
        down_whole.reshape((row_count, col_count) + down_momentum.shape)
        .transpose(2, 1, 3, 0, 4)
        .reshape(LAYERS, FF, D)
    )

    def own_block(whole, owner, first_start, second_start, first_size, second_size):
        direction = lax.cond(dp_index == owner, orthogonal, jnp.zeros_like, whole)
        block = lax.dynamic_slice(direction, (first_start, second_start), (first_size, second_size))
        block = share_block(block, owner)
        return block

    head_list, out_list, up_list, down_list = ([], [], [], [])
    for current_layer_index in range(LAYERS):
        members = []
        for member in range(3):
            block = own_block(
                head_whole[current_layer_index, member],
                (6 * current_layer_index + member) % dp_count,
                row_index * feature_span,
                col_index * head_width,
                feature_span,
                head_width,
            )
            members.append(
                head_projection_weights[current_layer_index, member]
                - muon_rate * D ** (-0.5) * block
            )
        head_list.append(jnp.stack(members))
        block = own_block(
            out_whole[current_layer_index],
            (6 * current_layer_index + 3) % dp_count,
            col_index * head_width,
            row_index * feature_span,
            head_width,
            feature_span,
        )
        out_list.append(
            output_projection_weights[current_layer_index] - muon_rate * (D // 16) ** (-0.5) * block
        )
        block = own_block(
            up_whole[current_layer_index],
            (6 * current_layer_index + 4) % dp_count,
            row_index * feature_span,
            col_index * hidden_span,
            feature_span,
            hidden_span,
        )
        up_list.append(up_projection_weights[current_layer_index] - muon_rate * D ** (-0.5) * block)
        block = own_block(
            down_whole[current_layer_index],
            (6 * current_layer_index + 5) % dp_count,
            col_index * hidden_span,
            row_index * feature_span,
            hidden_span,
            feature_span,
        )
        down_list.append(
            down_projection_weights[current_layer_index] - muon_rate * FF ** (-0.5) * block
        )
    first_moment = adam_first * norm_first + (1.0 - adam_first) * norm_sum
    second_moment = adam_second * norm_second + (1.0 - adam_second) * norm_sum * norm_sum
    corrected_first = first_moment / (1.0 - adam_first**STEP)
    corrected_second = second_moment / (1.0 - adam_second**STEP)
    norm_updated = norm_params - adam_rate * corrected_first / (
        jnp.sqrt(corrected_second) + adam_eps
    )
    return (
        hidden,
        grad_hidden,
        jnp.stack(head_list),
        jnp.stack(out_list),
        jnp.stack(up_list),
        jnp.stack(down_list),
        head_momentum,
        out_momentum,
        up_momentum,
        down_momentum,
        first_moment,
        second_moment,
        norm_updated,
    )


def solution(mesh):
    placed = (
        P("dp", "col", "row"),
        P("dp", None),
        P(None, None, "row", "col"),
        P(None, "col", "row"),
        P(None, "row", "col"),
        P(None, "col", "row"),
        P(None, None, "row", "col"),
        P(None, "col", "row"),
        P(None, "row", "col"),
        P(None, "col", "row"),
        P(None, None, "row"),
        P(None, None, "row"),
        P(None, None, "row"),
        P("dp", "col", "row"),
    )
    return jax.shard_map(
        on_device,
        mesh=mesh,
        in_specs=placed,
        out_specs=(
            P("dp", "col", "row"),
            P("dp", "col", "row"),
            P(None, None, "row", "col"),
            P(None, "col", "row"),
            P(None, "row", "col"),
            P(None, "col", "row"),
            P(None, None, "row", "col"),
            P(None, "col", "row"),
            P(None, "row", "col"),
            P(None, "col", "row"),
            P(None, None, "row"),
            P(None, None, "row"),
            P(None, None, "row"),
        ),
        check_vma=False,
    )
```

profile of v0, /device:TPU:0, one launch (start us, length us, event | category | flops | bytes accessed | tf_op | source)
XLA Modules:
  0.0 1137.3 jit_solution(9631978710469619161)
XLA Ops:
  18.2 24.7 %reduce-scatter.19.cloned.1.call-done = f32[1,256,192]{1,2,0:T(8,128)} async-done(((f32[1,1024,192]{1,2,0:T(8,128)}), f32[1,256,192]{1,2,0:T(8,128)}) %reduce-scatter.19.cloned.1.call-update) | async-done | bytes 196624 | tf_op jit(solution)/shard_map/reduce_scatter | solution.py:44
  79.2 19.4 %reduce-scatter.21.cloned.1.call-done = f32[1,256,64]{1,2,0:T(8,128)} async-done(((f32[1,1024,64]{1,2,0:T(8,128)}), f32[1,256,64]{1,2,0:T(8,128)}) %reduce-scatter.21.cloned.1.call-update) | async-done | bytes 65552 | tf_op jit(solution)/shard_map/reduce_scatter | solution.py:48
  127.6 26.0 %reduce-scatter.23.cloned.1.call-done = f32[1,256,256]{2,1,0:T(8,128)} async-done(((f32[1,1024,256]{2,1,0:T(8,128)}), f32[1,256,256]{2,1,0:T(8,128)}) %reduce-scatter.23.cloned.1.call-update) | async-done | bytes 262160 | tf_op jit(solution)/shard_map/reduce_scatter | solution.py:44
  155.9 26.7 %all-gather.14.cloned.1.call-done = f32[1,1024,256]{2,1,0:T(8,128)} async-done(((f32[1,256,256]{2,1,0:T(8,128)}), f32[1,1024,256]{2,1,0:T(8,128)}) %all-gather.14.cloned.1.call-update) | async-done | bytes 1048592 | tf_op jit(solution)/shard_map/all_gather | solution.py:40
  185.8 19.5 %reduce-scatter.25.cloned.1.call-done = f32[1,256,64]{1,2,0:T(8,128)} async-done(((f32[1,1024,64]{1,2,0:T(8,128)}), f32[1,256,64]{1,2,0:T(8,128)}) %reduce-scatter.25.cloned.1.call-update) | async-done | bytes 65552 | tf_op jit(solution)/shard_map/reduce_scatter | solution.py:48
  234.1 22.1 %reduce-scatter.27.cloned.1.call-done = f32[1,256,192]{1,2,0:T(8,128)} async-done(((f32[1,1024,192]{1,2,0:T(8,128)}), f32[1,256,192]{1,2,0:T(8,128)}) %reduce-scatter.27.cloned.1.call-update) | async-done | bytes 196624 | tf_op jit(solution)/shard_map/reduce_scatter | solution.py:44
  292.3 19.6 %reduce-scatter.29.cloned.1.call-done = f32[1,256,64]{1,2,0:T(8,128)} async-done(((f32[1,1024,64]{1,2,0:T(8,128)}), f32[1,256,64]{1,2,0:T(8,128)}) %reduce-scatter.29.cloned.1.call-update) | async-done | bytes 65552 | tf_op jit(solution)/shard_map/reduce_scatter | solution.py:48
  341.2 25.9 %reduce-scatter.31.cloned.1.call-done = f32[1,256,256]{2,1,0:T(8,128)} async-done(((f32[1,1024,256]{2,1,0:T(8,128)}), f32[1,256,256]{2,1,0:T(8,128)}) %reduce-scatter.31.cloned.1.call-update) | async-done | bytes 262160 | tf_op jit(solution)/shard_map/reduce_scatter | solution.py:44
  369.4 26.7 %all-gather.16.cloned.1.call-done = f32[1,1024,256]{2,1,0:T(8,128)} async-done(((f32[1,256,256]{2,1,0:T(8,128)}), f32[1,1024,256]{2,1,0:T(8,128)}) %all-gather.16.cloned.1.call-update) | async-done | bytes 1048592 | tf_op jit(solution)/shard_map/all_gather | solution.py:40
  399.2 19.7 %reduce-scatter.33.cloned.1.call-done = f32[1,256,64]{1,2,0:T(8,128)} async-done(((f32[1,1024,64]{1,2,0:T(8,128)}), f32[1,256,64]{1,2,0:T(8,128)}) %reduce-scatter.33.cloned.1.call-update) | async-done | bytes 65552 | tf_op jit(solution)/shard_map/reduce_scatter | solution.py:48
  459.6 24.5 %reduce-scatter.35.cloned.1.call-done = f32[1,256,256]{2,1,0:T(8,128)} async-done(((f32[1,1024,256]{2,1,0:T(8,128)}), f32[1,256,256]{2,1,0:T(8,128)}) %reduce-scatter.35.cloned.1.call-update) | async-done | bytes 262160 | tf_op jit(solution)/shard_map/reduce_scatter | solution.py:44
  486.0 26.7 %all-gather.18.cloned.1.call-done = f32[1,1024,256]{2,1,0:T(8,128)} async-done(((f32[1,256,256]{2,1,0:T(8,128)}), f32[1,1024,256]{2,1,0:T(8,128)}) %all-gather.18.cloned.1.call-update) | async-done | bytes 1048592 | tf_op jit(solution)/shard_map/all_gather | solution.py:40
  515.8 19.6 %reduce-scatter.37.cloned.1.call-done = f32[1,256,64]{1,2,0:T(8,128)} async-done(((f32[1,1024,64]{1,2,0:T(8,128)}), f32[1,256,64]{1,2,0:T(8,128)}) %reduce-scatter.37.cloned.1.call-update) | async-done | bytes 65552 | tf_op jit(solution)/shard_map/reduce_scatter | solution.py:48
  582.0 18.8 %reduce-scatter.41.cloned.1.call-done = f32[1,256,128]{1,2,0:T(8,128)} async-done(((f32[1,1024,128]{1,2,0:T(8,128)}), f32[1,256,128]{1,2,0:T(8,128)}) %reduce-scatter.41.cloned.1.call-update) | async-done | bytes 131088 | tf_op jit(solution)/shard_map/reduce_scatter | solution.py:44
  620.8 19.9 %reduce-scatter.43.cloned.1.call-done = f32[1,256,64]{1,2,0:T(8,128)} async-done(((f32[1,1024,64]{1,2,0:T(8,128)}), f32[1,256,64]{1,2,0:T(8,128)}) %reduce-scatter.43.cloned.1.call-update) | async-done | bytes 65552 | tf_op jit(solution)/shard_map/reduce_scatter | solution.py:48
  662.5 24.5 %reduce-scatter.45.cloned.1.call-done = f32[1,256,256]{2,1,0:T(8,128)} async-done(((f32[1,1024,256]{2,1,0:T(8,128)}), f32[1,256,256]{2,1,0:T(8,128)}) %reduce-scatter.45.cloned.1.call-update) | async-done | bytes 262160 | tf_op jit(solution)/shard_map/reduce_scatter | solution.py:44
  688.9 26.7 %all-gather.20.cloned.1.call-done = f32[1,1024,256]{2,1,0:T(8,128)} async-done(((f32[1,256,256]{2,1,0:T(8,128)}), f32[1,1024,256]{2,1,0:T(8,128)}) %all-gather.20.cloned.1.call-update) | async-done | bytes 1048592 | tf_op jit(solution)/shard_map/all_gather | solution.py:40
  807.0 18.1 %reduce-scatter.51.cloned.1.call-done = f32[1,256,128]{1,2,0:T(8,128)} async-done(((f32[1,1024,128]{1,2,0:T(8,128)}), f32[1,256,128]{1,2,0:T(8,128)}) %reduce-scatter.51.cloned.1.call-update) | async-done | bytes 131088 | tf_op jit(solution)/shard_map/reduce_scatter | solution.py:44
  826.0 19.5 %all_gather.83 = f32[1,1024,192]{1,2,0:T(8,128)S(1)} all-gather(f32[1,256,192]{1,2,0:T(8,128)S(1)} %pad_maximum_fusion.3), channel_id=1, replica_groups=mesh['dp'=2,'row'=4,'col'=4] {'row'}, dimensions={1}, use_global_device_ids=true | all-gather | bytes 983040 | tf_op jit(solution)/shard_map/all_gather | solution.py:40
  847.0 21.9 %all-gather.24.cloned.1.call-done = f32[32,64,256]{2,1,0:T(8,128)} async-done(((f32[2,64,256]{2,1,0:T(8,128)}), f32[32,64,256]{2,1,0:T(8,128)}) %all-gather.24.cloned.1.call-update) | async-done | bytes 2097168 | tf_op jit(solution)/shard_map/all_gather | solution.py:353
  925.1 52.5 %all-reduce.13.cloned.1.call-done = (f32[2,3,64,64]{2,3,1,0:T(8,128)}, f32[64,256]{1,0:T(8,128)}, f32[64,256]{1,0:T(8,128)}, f32[256,64]{0,1:T(8,128)}, f32[256,64]{0,1:T(8,128)}) async-done(((f32[2,3,64,64]{2,3,1,0:T(8,128)}, f32[64,256]{1,0:T(8,128)}, f32[64,256]{1,0:T(8,128)}, f32[256,64]{0,1:T(8,128)}, f32[256,64]{0,1:T(8,128)}), (f32[2,3,64,64]{2,3,1,0:T(8,128)}, f32[64,256]{1,0:T(8,128)}, ...) | async-done | bytes 360464 | tf_op jit(solution)/shard_map/psum | solution.py:341
  988.0 24.4 %all-gather.3 = f32[32,64,64]{2,1,0:T(8,128)S(1)} all-gather(f32[2,64,64]{2,1,0:T(8,128)S(1)} %multiply_add_fusion.21), channel_id=5, replica_groups=mesh['dp'=2,'row'=4,'col'=4] {'row','col'}, dimensions={0}, use_global_device_ids=true | all-gather | bytes 557056 | tf_op jit(solution)/shard_map/all_gather | solution.py:352
  1013.9 29.5 %psum.263 = f32[2,4,64]{2,1,0:T(4,128)S(1)} all-reduce(f32[2,4,64]{2,1,0:T(4,128)S(1)} %pad_maximum_fusion.12), channel_id=1, replica_groups=mesh['dp'=2,'row'=4,'col'=4] {'dp','col'}, use_global_device_ids=true, to_apply=%region_116.117 | all-reduce | flops 512 | bytes 4096 | tf_op jit(solution)/shard_map/psum | solution.py:345
  1106.1 21.1 %all-reduce.11.cloned.1.call-done = (f32[64,64]{1,0:T(8,128)}, f32[64,64]{1,0:T(8,128)}, f32[64,64]{1,0:T(8,128)}, f32[64,64]{1,0:T(8,128)}, f32[64,64]{1,0:T(8,...) async-done(((f32[64,64]{1,0:T(8,128)}, f32[64,64]{1,0:T(8,128)}, f32[64,64]{1,0:T(8,128)}, f32[64,64]{1,0:T(8,128)}, f32[64,64]{1,0:T(8,128)}, ...) | async-done | bytes 131088 | tf_op jit(solution)/shard_map/psum | solution.py:32
  (516 shorter events, 611.5 us)
Async XLA Ops:
  18.1 80.5 %reduce-scatter.21.cloned.1.call-start = ((), (), s32[]{:S(2)}) async-start(), calls=%async_computation.19 | async-start | bytes 327680 | tf_op jit(solution)/shard_map/reduce_scatter | solution.py:48
  79.1 74.5 %reduce-scatter.23.cloned.1.call-start = ((), (), s32[]{:S(2)}) async-start(), calls=%async_computation.20 | async-start | bytes 1310720 | tf_op jit(solution)/shard_map/reduce_scatter | solution.py:44
  127.6 55.0 %all-gather.14.cloned.1.call-start = ((), (), s32[]{:S(2)}) async-start(), calls=%async_computation.21 | async-start | bytes 1310720 | tf_op jit(solution)/shard_map/all_gather | solution.py:40
  155.9 49.5 %reduce-scatter.25.cloned.1.call-start = ((), (), s32[]{:S(2)}) async-start(), calls=%async_computation.22 | async-start | bytes 327680 | tf_op jit(solution)/shard_map/reduce_scatter | solution.py:48
  185.7 70.5 %reduce-scatter.27.cloned.1.call-start = ((), (), s32[]{:S(2)}) async-start(), calls=%async_computation.23 | async-start | bytes 983040 | tf_op jit(solution)/shard_map/reduce_scatter | solution.py:44
  234.1 77.8 %reduce-scatter.29.cloned.1.call-start = ((), (), s32[]{:S(2)}) async-start(), calls=%async_computation.24 | async-start | bytes 327680 | tf_op jit(solution)/shard_map/reduce_scatter | solution.py:48
  292.2 74.9 %reduce-scatter.31.cloned.1.call-start = ((), (), s32[]{:S(2)}) async-start(), calls=%async_computation.25 | async-start | bytes 1310720 | tf_op jit(solution)/shard_map/reduce_scatter | solution.py:44
  341.1 54.9 %all-gather.16.cloned.1.call-start = ((), (), s32[]{:S(2)}) async-start(), calls=%async_computation.26 | async-start | bytes 1310720 | tf_op jit(solution)/shard_map/all_gather | solution.py:40
  369.3 49.5 %reduce-scatter.33.cloned.1.call-start = ((), (), s32[]{:S(2)}) async-start(), calls=%async_computation.27 | async-start | bytes 327680 | tf_op jit(solution)/shard_map/reduce_scatter | solution.py:48
  399.1 85.0 %reduce-scatter.35.cloned.1.call-start = ((), (), s32[]{:S(2)}) async-start(), calls=%async_computation.28 | async-start | bytes 1310720 | tf_op jit(solution)/shard_map/reduce_scatter | solution.py:44
  459.5 53.1 %all-gather.18.cloned.1.call-start = ((), (), s32[]{:S(2)}) async-start(), calls=%async_computation.29 | async-start | bytes 1310720 | tf_op jit(solution)/shard_map/all_gather | solution.py:40
  515.8 57.7 %reduce-scatter.39.cloned.1.call-start = ((), (), s32[]{:S(2)}) async-start(), calls=%async_computation.31 | async-start | bytes 327680 | tf_op jit(solution)/shard_map/reduce_scatter | solution.py:44
  580.8 59.9 %reduce-scatter.43.cloned.1.call-start = ((), (), s32[]{:S(2)}) async-start(), calls=%async_computation.33 | async-start | bytes 327680 | tf_op jit(solution)/shard_map/reduce_scatter | solution.py:48
  620.8 66.2 %reduce-scatter.45.cloned.1.call-start = ((), (), s32[]{:S(2)}) async-start(), calls=%async_computation.34 | async-start | bytes 1310720 | tf_op jit(solution)/shard_map/reduce_scatter | solution.py:44
  662.4 53.1 %all-gather.20.cloned.1.call-start = ((), (), s32[]{:S(2)}) async-start(), calls=%async_computation.35 | async-start | bytes 1310720 | tf_op jit(solution)/shard_map/all_gather | solution.py:40
  688.8 49.6 %reduce-scatter.47.cloned.1.call-start = ((), (), s32[]{:S(2)}) async-start(), calls=%async_computation.36 | async-start | bytes 327680 | tf_op jit(solution)/shard_map/reduce_scatter | solution.py:48
  718.6 57.8 %reduce-scatter.49.cloned.1.call-start = ((), (), s32[]{:S(2)}) async-start(), calls=%async_computation.37 | async-start | bytes 327680 | tf_op jit(solution)/shard_map/reduce_scatter | solution.py:44
  764.1 61.0 %reduce-scatter.51.cloned.1.call-start = ((), (), s32[]{:S(2)}) async-start(), calls=%async_computation.38 | async-start | bytes 655360 | tf_op jit(solution)/shard_map/reduce_scatter | solution.py:44
  783.6 85.2 %all-gather.24.cloned.1.call-start = ((), (), s32[]{:S(2)}) async-start(), calls=%async_computation.41 | async-start | bytes 2228224 | tf_op jit(solution)/shard_map/all_gather | solution.py:353
  802.7 108.9 %all-gather.26.cloned.1.call-start = ((), (), s32[]{:S(2)}) async-start(), calls=%async_computation.42 | async-start | bytes 2228224 | tf_op jit(solution)/shard_map/all_gather | solution.py:354
  804.4 173.2 %all-reduce.13.cloned.1.call-start = ((), (), s32[]{:S(2)}) async-start(), calls=%async_computation.44 | async-start | bytes 917504 | tf_op jit(solution)/shard_map/psum | solution.py:341
  923.4 122.0 %reduce-scatter.53.cloned.1.call-start = ((), (), s32[]{:S(2)}) async-start(), calls=%async_computation.39 | async-start | bytes 327680 | tf_op jit(solution)/shard_map/reduce_scatter | solution.py:48
  924.9 126.5 %all-gather.22.cloned.1.call-start = ((), (), s32[]{:S(2)}) async-start(), calls=%async_computation.40 | async-start | bytes 3342336 | tf_op jit(solution)/shard_map/all_gather | solution.py:351
  979.4 147.8 %all-reduce.11.cloned.1.call-start = ((), (), s32[]{:S(2)}) async-start(), calls=%async_computation.43 | async-start | bytes 524288 | tf_op jit(solution)/shard_map/psum | solution.py:32
  (92 other events, 3769.9 us)
Sparse Core Ops, SparseCore 0:
  18.2 24.5 reduce-scatter.18
  127.7 25.8 reduce-scatter.22
  156.0 26.5 all-gather.13
  185.8 19.5 reduce-scatter.24
  234.2 21.9 reduce-scatter.26
  341.2 25.8 reduce-scatter.30
  369.4 26.5 all-gather.15
  399.3 19.5 reduce-scatter.32
  459.6 24.4 reduce-scatter.34
  486.0 26.5 all-gather.17
  515.9 19.5 reduce-scatter.36
  580.9 19.8 reduce-scatter.40
  620.9 19.8 reduce-scatter.42
  662.5 24.3 reduce-scatter.44
  688.9 26.5 all-gather.19
  718.8 19.5 reduce-scatter.46
  779.5 21.5 all-reduce.14
  803.4 21.6 reduce-scatter.50
  827.8 40.9 all-gather.23
  871.4 40.1 all-gather.25
  923.5 54.0 all-reduce.12
  980.1 20.4 reduce-scatter.52
  1003.3 48.0 all-gather.21
  1104.9 22.2 all-reduce.10
  (4 shorter events, 72.4 us)
where the time goes:
time: 1150 us; the launch traced here: 1140 us
  waiting for transfers between devices  579 us (50%)
  blocking collectives  332 us (29%)
  matrix products  116 us (10%)
  other arithmetic  57.6 us (5%)
  local copies, waits for them, and re-layouts  23.5 us (2%)
  between operations  15.9 us (1%)
  loops' own time  11.8 us (1%)
    reduce_scatter x10, waiting for transfers between devices, scatter_rows(): return lax.psum_scatter(values, 'row', scatter_dimension=1, tiled=True)  214 us
    reduce_scatter x8, waiting for transfers between devices, scatter_cols(): return lax.psum_scatter(values, 'col', scatter_dimension=1, tiled=True)  135 us
    psum x12, blocking collectives, feature_totals(): return lax.psum(values, 'row')  126 us
    all_gather x4, waiting for transfers between devices, gather_rows(): return lax.all_gather(values, 'row', axis=1, tiled=True)  107 us
    all_gather x6, blocking collectives, gather_rows(): return lax.all_gather(values, 'row', axis=1, tiled=True)  96.4 us
    psum x2, waiting for transfers between devices, on_device(): lax.psum((jnp.stack(head_grads), jnp.stack(out_grads), jnp.stack(up_grads...  70 us
    all_gather x8, blocking collectives, gather_cols(): return lax.all_gather(values, 'col', axis=1, tiled=True)  48.3 us
    psum x1, blocking collectives, on_device(): norm_sum = lax.psum(jnp.stack(norm_grads), ('dp', 'col'))  29.5 us
  transfers between devices with their start and end apart: 28, of which 27 were waited for; matrix products, arithmetic and copies ran while one was open for 6% of the time, Pallas kernels for 0%

commit v1 on v0

v1 whole, which is shorter than its diff:
```python
import functools
import math

import jax
import jax.numpy as jnp
from jax import lax
from jax.experimental import pallas as pl
from jax.experimental.pallas import tpu as pltpu
from jax.sharding import PartitionSpec as P

D = 256
FF = 1024
LAYERS = 2
NS_STEPS = 5
STEP = 10
HD = 64
TILE = 128

norm_eps = 1e-05
newton_coefs = (3.4445, -4.775, 2.0315)
frob_eps = 1e-07
muon_decay = 0.95
muon_rate = 0.5
adam_first = 0.9
adam_second = 0.999
adam_eps = 1e-08
adam_rate = 0.2
masked_score = -1e30

f32 = jnp.float32
bf16 = jnp.bfloat16

NN = (((1,), (0,)), ((), ()))
NT = (((1,), (1,)), ((), ()))
TN = (((0,), (0,)), ((), ()))


def dot(a, b, dims=NN):
    return lax.dot_general(a, b, dims, precision=lax.Precision.HIGH, preferred_element_type=f32)


def dot1(a, b, dims=NN):
    return lax.dot_general(a, b, dims, preferred_element_type=f32)


def low_lanes(rows):
    return lax.broadcasted_iota(jnp.int32, (rows, TILE), 1) < HD


def swap(t):
    return pltpu.roll(t, HD, 1)


def dup_low(t):
    return jnp.where(low_lanes(t.shape[0]), t, swap(t))


def dup_high(t):
    return jnp.where(low_lanes(t.shape[0]), swap(t), t)


def halves(t):
    high = t.astype(bf16)
    return high, (t - high.astype(f32)).astype(bf16)


def mixed(t):
    high = t.astype(bf16).astype(f32)
    return jnp.where(low_lanes(t.shape[0]), high, t - high).astype(bf16)


def high_only(t):
    return jnp.where(low_lanes(t.shape[0]), t, 0.0).astype(bf16)


def left_stack(t):
    m = mixed(t)
    return jnp.concatenate([m, m], axis=1)


def right_stack(t):
    high, low = halves(t)
    return jnp.concatenate([high, low], axis=1)


def normalize(values):
    mean = jnp.sum(values, axis=-1, keepdims=True) * (1.0 / D)
    center = values - mean
    variance = jnp.sum(center * center, axis=-1, keepdims=True) * (1.0 / D)
    inverse = lax.rsqrt(variance + norm_eps)
    return center * inverse, inverse


def normalize_back(grad_out, normed, inverse, gain):
    scaled = grad_out * gain
    first = jnp.sum(scaled, axis=-1, keepdims=True) * (1.0 / D)
    second = jnp.sum(scaled * normed, axis=-1, keepdims=True) * (1.0 / D)
    grad_in = inverse * (scaled - first - normed * second)
    gain_grad = jnp.sum(grad_out * normed, axis=0, keepdims=True)
    shift_grad = jnp.sum(grad_out, axis=0, keepdims=True)
    return grad_in, gain_grad, shift_grad


def attention_forward_kernel(
    first, rows, cols, idx_ref, h_ref, pack_ref, ln_ref, segrow_ref, segcol_ref,
    h_out, wkv_out, wqo_out, kv_out, qx_out, att_out, lse_out, mid_out, n1_out, i1_out, *extra
):
    c = idx_ref[0]
    span = mid_out.shape[0]
    for j in range(cols):
        for r in range(rows):
            piece = pack_ref[r * cols + j, 0:HD, :]
            wkv_out[r * HD:(r + 1) * HD, j * TILE:(j + 1) * TILE] = piece[:, :TILE]
            wqo_out[r * HD:(r + 1) * HD, j * TILE:(j + 1) * TILE] = piece[:, TILE:]
    if first:
        for j in range(cols):
            block = jnp.concatenate(
                [pack_ref[r * cols + j, HD:2 * HD, :] for r in range(rows)], axis=0
            )
            h_out[j] = jnp.transpose(block)
        (params_out,) = extra
        tiles = []
        for t in range(rows // 2):
            a = pack_ref[(2 * t) * cols, 2 * HD:2 * HD + 8, 0:TILE]
            b = pack_ref[(2 * t + 1) * cols, 2 * HD:2 * HD + 8, 0:TILE]
            tiles.append(jnp.where(low_lanes(8), a, swap(b)))
        params_out[...] = jnp.concatenate(tiles, axis=1)
        gain, shift = params_out[0:1, :], params_out[1:2, :]
        h_src = h_out
    else:
        h_src = h_ref
        gain, shift = ln_ref[4:5, :], ln_ref[5:6, :]
    wkv = wkv_out[...]
    for j in range(cols):
        kv_out[j * span:(j + 1) * span, :] = dot(h_src[j], wkv)
    h_own = h_src[c]
    qx_out[...] = dot(h_own, wqo_out[...])
    lane = lax.broadcasted_iota(jnp.int32, (span, TILE), 1)
    allowed = segcol_ref[c] == segrow_ref[...]
    lse_all = jnp.zeros((span, TILE), f32)
    for j in range(cols):
        tile = slice(j * TILE, (j + 1) * TILE)
        kv = kv_out[:, tile]
        k_right = right_stack(dup_low(kv))
        v_dup = dup_high(kv)
        v_mix = mixed(v_dup)
        v_high = high_only(v_dup)
        q_left = left_stack(dup_low(qx_out[:, tile]) * (HD ** -0.5))
        scores = jnp.where(allowed, dot1(q_left, k_right, NT), masked_score)
        top = jnp.max(scores, axis=-1, keepdims=True)
        raised = jnp.exp(scores - top)
        total = jnp.sum(raised, axis=-1, keepdims=True)
        p_high, p_low = halves(raised)
        out = dot1(p_high, v_mix) + dot1(p_low, v_high)
        out = (out + swap(out)) / total
        att_out[:, tile] = jnp.where(low_lanes(span), 0.0, out)
        lse_all = jnp.where(lane == j, top + jnp.log(total), lse_all)
    lse_out[...] = jnp.transpose(lse_all)[0:8, :]
    branch = dot(att_out[...], wqo_out[...], NT)
    normed, inverse = normalize(h_own + branch)
    n1_out[...] = normed
    i1_out[...] = jnp.broadcast_to(inverse, (span, TILE))
    mid_out[...] = normed * gain + shift


def feed_forward_kernel(
    layer, rows, cols, up_at, pack_ref, mid_ref, ln_ref,
    h_out, up_out, dn_out, before_out, act_out, n2_out, i2_out
):
    span = mid_ref.shape[0]
    for j in range(cols):
        for r in range(rows):
            at = (slice(r * HD, (r + 1) * HD), slice(j * 2 * TILE, (j + 1) * 2 * TILE))
            up_out[at] = pack_ref[r * cols + j, up_at:up_at + HD, :]
            dn_out[at] = pack_ref[r * cols + j, up_at + HD:up_at + 2 * HD, :]
    mid = mid_ref[...]
    before = dot(mid, up_out[...])
    before_out[...] = before
    activated = 0.5 * before * (1.0 + lax.erf(before * 0.7071067811865476))
    act_out[...] = activated
    feed = dot(activated, dn_out[...], NT)
    normed, inverse = normalize(mid + feed)
    n2_out[...] = normed
    i2_out[...] = jnp.broadcast_to(inverse, (span, TILE))
    h_out[...] = normed * ln_ref[4 * layer + 2:4 * layer + 3, :] + ln_ref[4 * layer + 3:4 * layer + 4, :]


def backward_kernel(
    layer, last, rows, cols, og_at, idx_ref, dh_ref, ln_ref, segrow_ref, segcol_ref, h_ref, wkv_ref, wqo_ref,
    kv_ref, qx_ref, att_ref, lse_ref, n1_ref, i1_ref, up_ref, dn_ref, before_ref, act_ref, n2_ref,
    i2_ref, dh_out, grad_out, dkv, dqx, dbef, dv1_ref, dv2_ref, norm_ref
):
    c = idx_ref[0]
    role = idx_ref[1]
    span = n1_ref.shape[0]
    gains = [ln_ref[4 * layer + k:4 * layer + k + 1, :] for k in range(4)]
    if last:
        block = jnp.concatenate([dh_ref[r * cols + c, og_at:og_at + HD, :] for r in range(rows)], axis=0)
        dh = jnp.transpose(block)
    else:
        dh = dh_ref[0]
        for j in range(1, cols):
            dh = dh + dh_ref[j]
    dv2, gain2, shift2 = normalize_back(dh, n2_ref[...], i2_ref[:, 0:1], gains[2])
    dv2_ref[...] = dv2
    d_act = dot(dv2, dn_ref[...])
    before = before_ref[...]
    slope = (
        0.5 * (1.0 + lax.erf(before * 0.7071067811865476))
        + before * jnp.exp(-0.5 * before * before) * 0.3989422804014327
    )
    dbef[...] = d_act * slope
    d_mid = dv2 + dot(dbef[...], up_ref[...], NT)
    dv1, gain1, shift1 = normalize_back(d_mid, n1_ref[...], i1_ref[:, 0:1], gains[0])
    dv1_ref[...] = dv1
    norm_ref[...] = jnp.zeros_like(norm_ref)
    for k, row in enumerate((gain1, shift1, gain2, shift2)):
        norm_ref[k:k + 1, :] = row
    d_att = dot(dv1, wqo_ref[...])
    lane = lax.broadcasted_iota(jnp.int32, (span, TILE), 1)
    inner_all = jnp.zeros((span, TILE), f32)
    for j in range(cols):
        tile = slice(j * TILE, (j + 1) * TILE)
        inner = jnp.sum(d_att[:, tile] * att_ref[:, tile], axis=-1, keepdims=True)
        inner_all = jnp.where(lane == j, inner, inner_all)
    inner_rows = jnp.transpose(inner_all)
    seg_row = segrow_ref[pl.ds(c, 1), :]
    low = low_lanes(span)
    for j in range(cols):
        tile = slice(j * TILE, (j + 1) * TILE)
        q_dup = dup_low(qx_ref[:, tile]) * (HD ** -0.5)
        q_mix = mixed(q_dup)
        q_left = jnp.concatenate([q_mix, q_mix], axis=1)
        q_high = high_only(q_dup)
        do_dup = dup_high(d_att[:, tile])
        do_mix = mixed(do_dup)
        do_left = jnp.concatenate([do_mix, do_mix], axis=1)
        do_high = high_only(do_dup)
        lse_row = lse_ref[j:j + 1, :]
        inner_row = inner_rows[j:j + 1, :]
        dq_t = jnp.zeros((TILE, span), f32)
        for b in range(cols):
            keys = slice(b * span, (b + 1) * span)
            kv = kv_ref[keys, tile]
            k_dup = dup_low(kv)
            v_dup = dup_high(kv)
            scores = dot1(right_stack(k_dup), q_left, NT)
            shares = jnp.where(segcol_ref[b] == seg_row, jnp.exp(scores - lse_row), 0.0)
            d_shares = dot1(right_stack(v_dup), do_left, NT)
            d_scores = shares * (d_shares - inner_row)
            p_high, p_low = halves(shares)
            s_high, s_low = halves(d_scores)
            dv = dot1(p_high, do_mix) + dot1(p_low, do_high)
            dk = dot1(s_high, q_mix) + dot1(s_low, q_high)
            dkv[keys, tile] = jnp.where(low, dk + swap(dk), dv + swap(dv))
            k_t = jnp.transpose(k_dup)
            k_t_high = k_t.astype(bf16)
            upper = lax.broadcasted_iota(jnp.int32, (TILE, span), 0) < HD
            k_t_mix = jnp.where(upper, k_t_high.astype(f32), k_t - k_t_high.astype(f32)).astype(bf16)
            k_t_only = jnp.where(upper, k_t, 0.0).astype(bf16)
            dq_t = dq_t + dot1(k_t_mix, s_high) + dot1(k_t_only, s_low)
        dq = jnp.transpose(dq_t)
        dqx[:, tile] = jnp.where(low, (dq + swap(dq)) * (HD ** -0.5), 0.0)
    wkv = wkv_ref[...]
    for j in range(cols):
        dh_out[j] = dot(dkv[j * span:(j + 1) * span, :], wkv, NT)
    dh_out[c] += dot(dqx[...], wqo_ref[...], NT) + dv1_ref[...]

    @pl.when(role == 0)
    def _():
        mid = n1_ref[...] * gains[0] + gains[1]
        for j in range(cols):
            grad_out[j] = dot(mid, dbef[:, j * 2 * TILE:(j + 1) * 2 * TILE], TN)

    @pl.when(role == 1)
    def _():
        for j in range(cols):
            grad_out[j] = dot(dv2_ref[...], act_ref[:, j * 2 * TILE:(j + 1) * 2 * TILE], TN)

    @pl.when(role == 2)
    def _():
        total = dot(h_ref[0], dkv[0:span, :], TN)
        for b in range(1, cols):
            total += dot(h_ref[b], dkv[b * span:(b + 1) * span, :], TN)
        for j in range(cols):
            grad_out[j, :, 0:TILE] = total[:, j * TILE:(j + 1) * TILE]
            grad_out[j, :, TILE:] = jnp.zeros((D, TILE), f32)

    @pl.when(role == 3)
    def _():
        total = dot(h_ref[c], dqx[...], TN) + dot(dv1_ref[...], att_ref[...], TN)
        norms = jnp.transpose(norm_ref[...])
        for j in range(cols):
            grad_out[j, :, 0:TILE] = total[:, j * TILE:(j + 1) * TILE]
            grad_out[j, :, TILE:] = norms


def newton_schulz(blocks):
    sizes = [jnp.sum(x * x, keepdims=True) for x in blocks]
    blocks = [x / (jnp.sqrt(s) + frob_eps) for x, s in zip(blocks, sizes)]
    for _ in range(NS_STEPS):
        grams = [dot(x, x, NT) for x in blocks]
        squares = [dot(a, a) for a in grams]
        polys = [newton_coefs[1] * a + newton_coefs[2] * s for a, s in zip(grams, squares)]
        blocks = [newton_coefs[0] * x + dot(p, x) for p, x in zip(polys, blocks)]
    return blocks


def orthogonal_kernel(cols, idx_ref, m_ref, out_ref, work):
    c = idx_ref[0]
    role = idx_ref[1]

    @pl.when(role < 2)
    def _():
        x = jnp.concatenate([m_ref[j] for j in range(cols)], axis=1)
        (x,) = newton_schulz([x])
        for j in range(cols):
            work[j] = x[:, j * 2 * TILE:(j + 1) * 2 * TILE] * math.sqrt(FF)
        out_ref[...] = work[c]

    @pl.when(role >= 2)
    def _():
        low = low_lanes(D)
        tiles = [m_ref[j, :, 0:TILE] for j in range(cols)]
        lefts, rights = [], []
        for t in range(cols // 2):
            a, b = tiles[2 * t], tiles[2 * t + 1]
            lefts.append(jnp.where(low, a, swap(b)))
            rights.append(jnp.where(low, swap(a), b))
        left, right = newton_schulz(
            [jnp.concatenate(lefts, axis=1), jnp.concatenate(rights, axis=1)]
        )
        for t in range(cols // 2):
            a = left[:, t * TILE:(t + 1) * TILE] * math.sqrt(D)
            b = right[:, t * TILE:(t + 1) * TILE] * math.sqrt(D)
            work[2 * t, :, 0:TILE] = jnp.where(low, a, swap(b))
            work[2 * t + 1, :, 0:TILE] = jnp.where(low, swap(a), b)
        out_ref[:, 0:TILE] = work[c, :, 0:TILE]
        out_ref[:, TILE:] = jnp.zeros((D, TILE), f32)


def call(body, operands, outs, scratch=(), flops=0):
    specs = [pl.BlockSpec(memory_space=pltpu.SMEM if x.ndim == 1 else pltpu.VMEM) for x in operands]
    moved = sum(4 * math.prod(x.shape) for x in operands) + sum(4 * math.prod(s) for s in outs)
    return pl.pallas_call(
        body,
        out_shape=[jax.ShapeDtypeStruct(s, f32) for s in outs],
        in_specs=specs,
        out_specs=[pl.BlockSpec(memory_space=pltpu.VMEM) for _ in outs],
        scratch_shapes=[pltpu.VMEM(s, f32) for s in scratch],
        compiler_params=pltpu.CompilerParams(vmem_limit_bytes=50 * 2**20),
        cost_estimate=pl.CostEstimate(flops=flops, bytes_accessed=moved, transcendentals=0),
    )(*operands)


def on_device(
    layer_input,
    segment_ids,
    head_projection_weights,
    output_projection_weights,
    up_projection_weights,
    down_projection_weights,
    head_moment,
    out_moment,
    up_moment,
    down_moment,
    norm_params,
    norm_first,
    norm_second,
    output_grad,
):
    row = lax.axis_index("row").astype(jnp.int32)
    col = lax.axis_index("col").astype(jnp.int32)
    rows = lax.axis_size("row")
    cols = lax.axis_size("col")
    dps = lax.axis_size("dp")
    span = layer_input.shape[1]
    length = span * cols
    idx = jnp.stack([col, row])
    swap2 = lambda x: jnp.swapaxes(x, -1, -2)

    def attention_pack(heads, outs):
        return jnp.concatenate([heads[1], heads[2], heads[0], swap2(outs)], axis=1)

    params = jnp.pad(norm_params.reshape(8, HD), ((0, 0), (0, 2 * TILE - HD)))
    shards = (
        jnp.concatenate(
            [
                attention_pack(head_projection_weights[0], output_projection_weights[0]),
                swap2(layer_input[0]),
                params,
            ]
        ),
        jnp.concatenate([up_projection_weights[0], swap2(down_projection_weights[0])]),
        jnp.concatenate(
            [
                attention_pack(head_projection_weights[1], output_projection_weights[1]),
                up_projection_weights[1],
                swap2(down_projection_weights[1]),
                swap2(output_grad[0]),
            ]
        ),
    )
    pack_a, pack_f, pack_b = [lax.all_gather(s, ("row", "col"), axis=0) for s in shards]
    seg_row = segment_ids.reshape(1, length)
    seg_rows = segment_ids.reshape(cols, span)
    seg_col = segment_ids.reshape(cols, span, 1)

    moments = []
    for l in range(LAYERS):
        blank = jnp.zeros((HD, TILE), f32)
        heads = head_moment[l]
        moments.append(
            jnp.stack(
                [
                    up_moment[l],
                    swap2(down_moment[l]),
                    jnp.concatenate([heads[1], heads[2], blank], axis=1),
                    jnp.concatenate([heads[0], swap2(out_moment[l]), blank], axis=1),
                ]
            )
        )
    moments = lax.all_to_all(jnp.stack(moments, axis=1), "row", 0, 0, tiled=True)

    full = (cols, span, D)
    own = (span, D)
    wide = (span, FF)
    half = (D, cols * TILE)
    one = (span, TILE)
    kept = []
    hidden = jnp.zeros((8, TILE), f32)
    ln = jnp.zeros((8, TILE), f32)
    for l in range(LAYERS):
        first = l == 0
        outs = [full if first else (8, TILE), half, half, (length, cols * TILE), (span, cols * TILE),
                (span, cols * TILE), (8, span), own, own, one]
        if first:
            outs.append((8, D))
        got = call(
            functools.partial(attention_forward_kernel, first, rows, cols),
            [idx, hidden, pack_a if first else pack_b, ln, seg_row, seg_col],
            outs, flops=5 * 10**9,
        )
        h_full, wkv, wqo, kv, qx, att, lse, mid, n1, i1 = got[:10]
        if first:
            ln = got[10]
        else:
            h_full = hidden
        h_own, up, dn, before, act, n2, i2 = call(
            functools.partial(feed_forward_kernel, l, rows, cols, 0 if first else HD),
            [pack_f if first else pack_b, mid, ln],
            [own, (D, FF), (D, FF), wide, wide, own, one], flops=10**9,
        )
        kept.append((h_full, wkv, wqo, kv, qx, att, lse, n1, i1, up, dn, before, act, n2, i2))
        if l + 1 < LAYERS:
            hidden = lax.all_gather(h_own, "col", axis=0)
    layer_output = lax.dynamic_slice(h_own, (0, row * HD), (span, HD))[None]

    swap_pairs = [(0, 1), (1, 0)]
    reduced = [None] * LAYERS
    dh = pack_b
    for l in reversed(range(LAYERS)):
        last = l == LAYERS - 1
        dh_part, grads = call(
            functools.partial(backward_kernel, l, last, rows, cols, 3 * HD),
            [idx, dh, ln, seg_rows, seg_col] + list(kept[l]),
            [full, (cols, D, D)],
            [(length, cols * TILE), (span, cols * TILE), wide, own, own, (TILE, D)], flops=12 * 10**9,
        )
        dh = lax.all_to_all(dh_part, "col", 0, 0, tiled=True)
        mine = lax.psum_scatter(grads, "col", scatter_dimension=0, tiled=False)
        mine = mine + lax.ppermute(mine, "dp", swap_pairs) if dps == 2 else lax.psum(mine, "dp")
        mine = mine + muon_decay * moments[:, l].reshape(D, D)
        whole = lax.all_gather(mine, "col", axis=0)
        (direction,) = call(
            functools.partial(orthogonal_kernel, cols),
            [idx, whole], [(D, D)], [(cols, D, D)], flops=3 * 10**9,
        )
        sent = jnp.concatenate([mine.reshape(rows, HD, D), direction.reshape(rows, HD, D)], axis=1)
        reduced[l] = lax.all_to_all(sent, "row", 0, 0, tiled=True)
    dh = jnp.sum(dh, axis=0)
    input_grad = lax.dynamic_slice(dh, (0, row * HD), (span, HD))[None]

    head_new, out_new, up_new, down_new = [], [], [], []
    head_mom, out_mom, up_mom, down_mom, norm_sum = [], [], [], [], []
    for l in range(LAYERS):
        mom, step = reduced[l][:, :HD], reduced[l][:, HD:] * muon_rate
        parts = lambda x: (jnp.stack([x[3, :, :HD], x[2, :, :HD], x[2, :, HD:TILE]]), swap2(x[3, :, HD:TILE]))
        heads, outs = parts(mom)
        head_mom.append(heads)
        out_mom.append(outs)
        up_mom.append(mom[0])
        down_mom.append(swap2(mom[1]))
        norm_sum.append(swap2(mom[3, :, TILE:TILE + 4]))
        heads, outs = parts(step)
        head_new.append(head_projection_weights[l] - D ** -0.5 * heads)
        out_new.append(output_projection_weights[l] - (D // 16) ** -0.5 * outs)
        up_new.append(up_projection_weights[l] - D ** -0.5 * step[0])
        down_new.append(down_projection_weights[l] - FF ** -0.5 * swap2(step[1]))
    norm_sum = jnp.stack(norm_sum)
    first_moment = adam_first * norm_first + (1.0 - adam_first) * norm_sum
    second_moment = adam_second * norm_second + (1.0 - adam_second) * norm_sum * norm_sum
    corrected_first = first_moment / (1.0 - adam_first**STEP)
    corrected_second = second_moment / (1.0 - adam_second**STEP)
    norm_updated = norm_params - adam_rate * corrected_first / (
        jnp.sqrt(corrected_second) + adam_eps
    )
    return (
        layer_output,
        input_grad,
        jnp.stack(head_new),
        jnp.stack(out_new),
        jnp.stack(up_new),
        jnp.stack(down_new),
        jnp.stack(head_mom),
        jnp.stack(out_mom),
        jnp.stack(up_mom),
        jnp.stack(down_mom),
        first_moment,
        second_moment,
        norm_updated,
    )


def solution(mesh):
    placed = (
        P("dp", "col", "row"),
        P("dp", None),
        P(None, None, "row", "col"),
        P(None, "col", "row"),
        P(None, "row", "col"),
        P(None, "col", "row"),
        P(None, None, "row", "col"),
        P(None, "col", "row"),
        P(None, "row", "col"),
        P(None, "col", "row"),
        P(None, None, "row"),
        P(None, None, "row"),
        P(None, None, "row"),
        P("dp", "col", "row"),
    )
    return jax.shard_map(
        on_device,
        mesh=mesh,
        in_specs=placed,
        out_specs=(
            P("dp", "col", "row"),
            P("dp", "col", "row"),
            P(None, None, "row", "col"),
            P(None, "col", "row"),
            P(None, "row", "col"),
            P(None, "col", "row"),
            P(None, None, "row", "col"),
            P(None, "col", "row"),
            P(None, "row", "col"),
            P(None, "col", "row"),
            P(None, None, "row"),
            P(None, None, "row"),
            P(None, None, "row"),
        ),
        check_vma=False,
    )
```

time: 1150 us -> 358 us (0.31)
  waiting for transfers between devices: 579 us -> 194 us
  blocking collectives: 332 us -> 0 us
  matrix products: 116 us -> 0 us
  Pallas kernels: 0 us -> 74.1 us
  other arithmetic: 57.6 us -> 16.6 us
  starting transfers between devices: 1.17 us -> 24.7 us
  loops' own time: 11.8 us -> 0 us
    reduce_scatter x18 -> x2, waiting for transfers between devices: 349 us -> 2.33 us  [on_device(): mine = lax.psum_scatter(grads, 'col', scatter_dimension=0, tiled=False)]
    all_gather x15 -> x0, blocking collectives: 169 us -> none  [the longest x6 96.4 us: gather_rows(): return lax.all_gather(values, 'row', axis=1, tiled=True)]
    psum x14 -> x0, blocking collectives: 163 us -> none  [the longest x12 126 us: feature_totals(): return lax.psum(values, 'row')]
    dot_general x126 -> x0, matrix products: 116 us -> none  [the longest x30 23.4 us: orthogonal(): jnp.dot(polynomial, current, precision=highest_precision)]
    psum x3 -> x0, waiting for transfers between devices: 91 us -> none  [the longest x2 70 us: on_device(): lax.psum((jnp.stack(head_grads), jnp.stack(out_grads), jnp.stack(up_grads...]
    pallas_call x0 -> x8, Pallas kernels: none -> 74.1 us  [call(): pl.pallas_call(body, out_shape=[jax.ShapeDtypeStruct(s, f32) for s in out...]
    all_to_all x0 -> x5, waiting for transfers between devices: none -> 39.1 us  [the longest x2 14.5 us: on_device(): reduced[l] = lax.all_to_all(sent, 'row', 0, 0, tiled=True)]
    all_to_all x0 -> x5, starting transfers between devices: none -> 20.5 us  [the longest x2 8.83 us: on_device(): reduced[l] = lax.all_to_all(sent, 'row', 0, 0, tiled=True)]
  transfers between devices with their start and end apart: 28 -> 15, of which waited for: 27 -> 11; matrix products, arithmetic and copies ran while one was open for 6% -> 6% of each run, Pallas kernels for 0% -> 12%
where the time goes in v1:
time: 358 us; the launch traced here: 351 us
  waiting for transfers between devices  194 us (54%)
  Pallas kernels  74.1 us (21%)
  local copies, waits for them, and re-layouts  26.4 us (7%)
  starting transfers between devices  24.7 us (7%)
  other arithmetic  16.6 us (5%)
  between operations  14.8 us (4%)
    all_gather x3, waiting for transfers between devices, on_device(): lax.all_gather(s, ('row', 'col'), axis=0)  127 us
    pallas_call x8, Pallas kernels, call(): pl.pallas_call(body, out_shape=[jax.ShapeDtypeStruct(s, f32) for s in out...  74.1 us
    all_to_all x2, waiting for transfers between devices, on_device(): reduced[l] = lax.all_to_all(sent, 'row', 0, 0, tiled=True)  14.5 us
    unnamed x69, local copies, waits for them, and re-layouts  14.5 us
    all_to_all x2, waiting for transfers between devices, on_device(): dh = lax.all_to_all(dh_part, 'col', 0, 0, tiled=True)  13.2 us
    all_gather x1, waiting for transfers between devices, on_device(): hidden = lax.all_gather(h_own, 'col', axis=0)  12.5 us
    all_to_all x1, waiting for transfers between devices, on_device(): lax.all_to_all(jnp.stack(moments, axis=1), 'row', 0, 0, tiled=True)  11.4 us
    all_to_all x2, starting transfers between devices, on_device(): reduced[l] = lax.all_to_all(sent, 'row', 0, 0, tiled=True)  8.83 us
  transfers between devices with their start and end apart: 15, of which 11 were waited for; matrix products, arithmetic and copies ran while one was open for 6% of the time, Pallas kernels for 12%

profile of v1, /device:TPU:0, one launch (start us, length us, event | category | flops | bytes accessed | tf_op | source)
XLA Modules:
  0.0 351.0 jit_solution(18128929958215181848)
XLA Ops:
  16.7 39.8 %all-gather.17.cloned.1.call-done = f32[2176,256]{1,0:T(8,128)} async-done(((f32[136,256]{1,0:T(8,128)}), f32[2176,256]{1,0:T(8,128)}) %all-gather.17.cloned.1.call-update) | async-done | bytes 2228240 | tf_op jit(solution)/shard_map/all_gather | solution.py:404
  56.5 6.8 %shard_map.237 = (f32[4,256,256]{2,1,0:T(8,128)}, f32[256,512]{1,0:T(8,128)S(1)}, f32[256,512]{1,0:T(8,128)S(1)}, f32[1024,512]{1,0:T(8,128)}, f32[256,512]{1,0:...) custom-call(s32[2]{0:T(128)S(1)} %pad_add_fusion.idx_ref, ...), custom_call_target="tpu_custom_call" | custom-call | flops 5000000000 | bytes 8159240 | tf_op jit(solution)/shard_map/pallas_call | solution.py:345
  64.7 34.8 %all-gather.15.cloned.1.call-done = f32[2048,256]{1,0:T(8,128)} async-done(((f32[128,256]{1,0:T(8,128)}), f32[2048,256]{1,0:T(8,128)}) %all-gather.15.cloned.1.call-update) | async-done | bytes 2097168 | tf_op jit(solution)/shard_map/all_gather | solution.py:404
  99.5 3.9 %shard_map.238 = (f32[256,256]{1,0:T(8,128)}, f32[256,1024]{1,0:T(8,128)S(1)}, f32[256,1024]{1,0:T(8,128)S(1)}, f32[256,1024]{1,0:T(8,128)S(1)}, f32[256,1024]{1...) custom-call(f32[16,128,256]{2,1,0:T(8,128)} %bitcast.222, f32[256,256]{1,0:T(8,128)S(1)} %get-tuple-element.51.mid_ref, ...), custom_call_target="tpu_custom_call" | custom-call | flops 1000000000 | bytes 7217152 | tf_op jit(solution)/shard_map/pallas_call | solution.py:345
  109.6 12.5 %all-gather.19.cloned.1.call-done = f32[1024,256]{1,0:T(8,128)} async-done(((f32[256,256]{1,0:T(8,128)}), f32[1024,256]{1,0:T(8,128)}) %all-gather.19.cloned.1.call-update) | async-done | bytes 1048592 | tf_op jit(solution)/shard_map/all_gather | solution.py:456
  122.1 52.6 %all-gather.13.cloned.1.call-done = f32[4096,256]{1,0:T(8,128)} async-done(((f32[256,256]{1,0:T(8,128)}), f32[4096,256]{1,0:T(8,128)}) %all-gather.13.cloned.1.call-update) | async-done | bytes 4194320 | tf_op jit(solution)/shard_map/all_gather | solution.py:404
  174.7 9.0 %shard_map.239 = (f32[8,128]{1,0:T(8,128)}, f32[256,512]{1,0:T(8,128)S(1)}, f32[256,512]{1,0:T(8,128)S(1)}, f32[1024,512]{1,0:T(8,128)}, f32[256,512]{1,0:T(8,12...) custom-call(s32[2]{0:T(128)S(1)} %pad_add_fusion.idx_ref, ...), custom_call_target="tpu_custom_call" | custom-call | flops 5000000000 | bytes 10121224 | tf_op jit(solution)/shard_map/pallas_call | solution.py:345
  183.7 4.2 %shard_map.240 = (f32[256,256]{1,0:T(8,128)S(1)}, f32[256,1024]{1,0:T(8,128)S(1)}, f32[256,1024]{1,0:T(8,128)S(1)}, f32[256,1024]{1,0:T(8,128)S(1)}, f32[256,102...) custom-call(f32[16,256,256]{2,1,0:T(8,128)} %bitcast.206, f32[256,256]{1,0:T(8,128)S(1)} %get-tuple-element.54.mid_ref, ...), custom_call_target="tpu_custom_call" | custom-call | flops 1000000000 | bytes 9314304 | tf_op jit(solution)/shard_map/pallas_call | solution.py:345
  190.9 15.7 %shard_map.241 = (f32[4,256,256]{2,1,0:T(8,128)}, f32[4,256,256]{2,1,0:T(8,128)}) custom-call(s32[2]{0:T(128)S(1)} %pad_add_fusion.idx_ref, f32[16,256,256]{2,1,0:T(8,128)} %bitcast.207, f32[8,256]{1,0:T(8,128)S(1)} %get-tuple-element.52.ln_ref, s32[4,256]{1,0:T(4,128)S(1)} %reshape.169.segrow_ref, s32[4,256,1]{2,1,0:T(8,128)S(1)} %reshape.180.segcol_ref, ...), custom_call_target="tpu_custom_call" | custom-call | flops 12000000000 | bytes 16539656 | tf_op jit(solution)/shard_map/pallas_call | solution.py:345
  206.6 4.4 %all-to-all-start = ((f32[4,256,256]{2,1,0:T(8,128)}), f32[4,256,256]{2,1,0:T(8,128)}, u32[]{:S(2)}, u32[]{:S(2)}) async-start(f32[4,256,256]{2,1,0:T(8,128)} %get-tuple-element.70), calls=%async_computation | async-start | bytes 2097152 | tf_op jit(solution)/shard_map/all_to_all | solution.py:470
  214.1 13.2 %all-to-all-done.dh_ref = f32[4,256,256]{2,1,0:T(8,128)} async-done(((f32[4,256,256]{2,1,0:T(8,128)}), f32[4,256,256]{2,1,0:T(8,128)}, u32[]{:S(2)}, u32[]{:S(2)}) %all-to-all-start) | async-done | bytes 1048608 | tf_op jit(solution)/shard_map/all_to_all | solution.py:470
  228.9 14.4 %shard_map.242 = (f32[4,256,256]{2,1,0:T(8,128)}, f32[4,256,256]{2,1,0:T(8,128)}) custom-call(s32[2]{0:T(128)S(1)} %pad_add_fusion.idx_ref, f32[4,256,256]{2,1,0:T(8,128)} %all-to-all-done.dh_ref, f32[8,256]{1,0:T(8,128)S(1)} %get-tuple-element.52.ln_ref, s32[4,256]{1,0:T(4,128)S(1)} %reshape.169.segrow_ref, s32[4,256,1]{2,1,0:T(8,128)S(1)} %reshape.180.segcol_ref, ...), custom_call_target="tpu_custom_call" | custom-call | flops 12000000000 | bytes 13393928 | tf_op jit(solution)/shard_map/pallas_call | solution.py:345
  246.3 3.7 %all-to-all-start.2 = ((f32[4,2,64,256]{3,2,1,0:T(8,128)}), f32[4,2,64,256]{3,2,1,0:T(8,128)S(1)}, u32[]{:S(2)}, u32[]{:S(2)}) async-start(f32[4,2,64,256]{3,2,1,0:T(8,128)} %pad_maximum_fusion), calls=%async_computation.3 | async-start | bytes 1048576 | tf_op jit(solution)/shard_map/all_to_all | solution.py:423
  252.0 11.4 %all-to-all-done.2 = f32[4,2,64,256]{3,2,1,0:T(8,128)S(1)} async-done(((f32[4,2,64,256]{3,2,1,0:T(8,128)}), f32[4,2,64,256]{3,2,1,0:T(8,128)S(1)}, u32[]{:S(2)}, u32[]{:S(2)}) %all-to-all-start.2) | async-done | bytes 524320 | tf_op jit(solution)/shard_map/all_to_all | solution.py:423
  263.4 1.7 bitcast_add_fusion
  265.2 2.3 reduce-scatter.3.cloned.1.call-done
  269.0 6.8 %collective-permute-done = f32[256,256]{1,0:T(8,128)S(1)} collective-permute-done((f32[256,256]{1,0:T(8,128)}, f32[256,256]{1,0:T(8,128)S(1)}, u32[]{:S(2)}, u32[]{:S(2)}) %collective-permute-start) | collective-permute-done | bytes 262176 | tf_op jit(solution)/shard_map/ppermute | solution.py:472
  277.5 3.5 %all-to-all-start.1 = ((f32[4,256,256]{2,1,0:T(8,128)}), f32[4,256,256]{2,1,0:T(8,128)S(1)}, u32[]{:S(2)}, u32[]{:S(2)}) async-start(f32[4,256,256]{2,1,0:T(8,128)} %get-tuple-element.86), calls=%async_computation.1 | async-start | bytes 2097152 | tf_op jit(solution)/shard_map/all_to_all | solution.py:470
  281.1 4.9 %all-gather.23.cloned.1.call-done = f32[1024,256]{1,0:T(8,128)} async-done(((f32[256,256]{1,0:T(8,128)}), f32[1024,256]{1,0:T(8,128)}) %all-gather.23.cloned.1.call-update) | async-done | bytes 1048592 | tf_op jit(solution)/shard_map/all_gather | solution.py:474
  287.2 9.9 %shard_map.244 = f32[256,256]{1,0:T(8,128)S(1)} custom-call(s32[2]{0:T(128)S(1)} %pad_add_fusion.idx_ref, f32[4,256,256]{2,1,0:T(8,128)S(1)} %bitcast.204), custom_call_target="tpu_custom_call" | custom-call | flops 3000000000 | bytes 1310728 | tf_op jit(solution)/shard_map/pallas_call | solution.py:345
  298.0 3.5 all-to-all-start.4
  305.9 10.3 %shard_map.243 = f32[256,256]{1,0:T(8,128)S(1)} custom-call(s32[2]{0:T(128)S(1)} %pad_add_fusion.idx_ref, f32[4,256,256]{2,1,0:T(8,128)S(1)} %bitcast.203), custom_call_target="tpu_custom_call" | custom-call | flops 3000000000 | bytes 1310728 | tf_op jit(solution)/shard_map/pallas_call | solution.py:345
  317.1 5.4 %all-to-all-start.3 = ((f32[4,128,256]{2,1,0:T(8,128)}), f32[4,128,256]{2,1,0:T(8,128)S(1)}, u32[]{:S(2)}, u32[]{:S(2)}) async-start(f32[4,128,256]{2,1,0:T(8,128)} %pad_maximum_fusion.1), calls=%async_computation.4 | async-start | bytes 1048576 | tf_op jit(solution)/shard_map/all_to_all | solution.py:480
  322.8 14.5 %all-to-all-done.3 = f32[4,128,256]{2,1,0:T(8,128)S(1)} async-done(((f32[4,128,256]{2,1,0:T(8,128)}), f32[4,128,256]{2,1,0:T(8,128)S(1)}, u32[]{:S(2)}, u32[]{:S(2)}) %all-to-all-start.3) | async-done | bytes 524320 | tf_op jit(solution)/shard_map/all_to_all | solution.py:480
  (150 shorter events, 47.2 us)
Async XLA Ops:
  7.2 49.3 %copy-start = (s32[1,1024]{1,0:T(1,128)S(1)}, s32[1,1024]{1,0:T(1,128)}, u32[]{:S(2)}) copy-start(s32[1,1024]{1,0:T(1,128)} %segrow_ref.3) | copy-start | bytes 12292
  7.2 49.3 %all-gather.17.cloned.1.call-start = ((), (), s32[]{:S(2)}) async-start(), calls=%async_computation.11 | async-start | bytes 2367488 | tf_op jit(solution)/shard_map/all_gather | solution.py:404
  10.2 46.3 %copy-start.22 = (f32[1,64,64]{1,2,0:T(8,128)}, f32[1,64,64]{1,2,0:T(8,128)S(1)}, u32[]{:S(2)}) copy-start(f32[1,64,64]{1,2,0:T(8,128)S(1)} %copy.149) | copy-start | bytes 49156
  11.8 87.7 %all-gather.15.cloned.1.call-start = ((), (), s32[]{:S(2)}) async-start(), calls=%async_computation.10 | async-start | bytes 2228224 | tf_op jit(solution)/shard_map/all_gather | solution.py:404
  14.3 107.7 %all-gather.19.cloned.1.call-start = ((), (), s32[]{:S(2)}) async-start(), calls=%async_computation.12 | async-start | bytes 1310720 | tf_op jit(solution)/shard_map/all_gather | solution.py:456
  64.7 44.2 %copy-start.13 = (f32[8,256]{1,0:T(8,128)}, f32[8,256]{1,0:T(8,128)S(1)}, u32[]{:S(2)}) copy-start(f32[8,256]{1,0:T(8,128)S(1)} %get-tuple-element.77.lse_ref) | copy-start | bytes 24580
  106.4 68.3 %all-gather.13.cloned.1.call-start = ((), (), s32[]{:S(2)}) async-start(), calls=%async_computation.9 | async-start | bytes 4456448 | tf_op jit(solution)/shard_map/all_gather | solution.py:404
  107.3 76.4 %copy-start.20 = (f32[1,64,64]{1,2,0:T(8,128)}, f32[1,64,64]{1,2,0:T(8,128)S(1)}, u32[]{:S(2)}) copy-start(f32[1,64,64]{1,2,0:T(8,128)S(1)} %copy.148) | copy-start | bytes 49156
  109.0 141.5 %reduce-scatter.5.cloned.1.call-start = ((), (), s32[]{:S(2)}) async-start(), calls=%async_computation.8 | async-start | bytes 1310720 | tf_op jit(solution)/shard_map/reduce_scatter | solution.py:471
  206.5 20.8 %copy-start.10 = (f32[256,256]{1,0:T(8,128)S(1)}, f32[256,256]{1,0:T(8,128)}, u32[]{:S(2)}) copy-start(f32[256,256]{1,0:T(8,128)} %copy-done.9) | copy-start | bytes 786436
  206.6 20.7 %all-to-all-start = ((f32[4,256,256]{2,1,0:T(8,128)}), f32[4,256,256]{2,1,0:T(8,128)}, u32[]{:S(2)}, u32[]{:S(2)}) async-start(f32[4,256,256]{2,1,0:T(8,128)} %get-tuple-element.70), calls=%async_computation | async-start | bytes 2097152 | tf_op jit(solution)/shard_map/all_to_all | solution.py:470
  211.0 56.6 %reduce-scatter.3.cloned.1.call-start = ((), (), s32[]{:S(2)}) async-start(), calls=%async_computation.7 | async-start | bytes 1310720 | tf_op jit(solution)/shard_map/reduce_scatter | solution.py:471
  246.3 17.1 %all-to-all-start.2 = ((f32[4,2,64,256]{3,2,1,0:T(8,128)}), f32[4,2,64,256]{3,2,1,0:T(8,128)S(1)}, u32[]{:S(2)}, u32[]{:S(2)}) async-start(f32[4,2,64,256]{3,2,1,0:T(8,128)} %pad_maximum_fusion), calls=%async_computation.3 | async-start | bytes 1048576 | tf_op jit(solution)/shard_map/all_to_all | solution.py:423
  250.0 36.0 %all-gather.23.cloned.1.call-start = ((), (), s32[]{:S(2)}) async-start(), calls=%async_computation.14 | async-start | bytes 1310720 | tf_op jit(solution)/shard_map/all_gather | solution.py:474
  250.5 13.0 %collective-permute-start.1 = (f32[256,256]{1,0:T(8,128)}, f32[256,256]{1,0:T(8,128)S(1)}, u32[]{:S(2)}, u32[]{:S(2)}) collective-permute-start(f32[256,256]{1,0:T(8,128)} %bitcast.212), channel_id=1, source_target_pairs={{0,16},{16,0},{1,17},{17,1},{2,18},{18,2},{3,19},{19,3},{4,20},{20... | collective-permute-start | bytes 786440 | tf_op jit(solution)/shard_map/ppermute | solution.py:472
  265.2 39.5 %all-gather.21.cloned.1.call-start = ((), (), s32[]{:S(2)}) async-start(), calls=%async_computation.13 | async-start | bytes 1310720 | tf_op jit(solution)/shard_map/all_gather | solution.py:474
  267.5 8.3 %collective-permute-start = (f32[256,256]{1,0:T(8,128)}, f32[256,256]{1,0:T(8,128)S(1)}, u32[]{:S(2)}, u32[]{:S(2)}) collective-permute-start(f32[256,256]{1,0:T(8,128)} %bitcast.213), channel_id=1, source_target_pairs={{0,16},{16,0},{1,17},{17,1},{2,18},{18,2},{3,19},{19,3},{4,20},{20... | collective-permute-start | bytes 786440 | tf_op jit(solution)/shard_map/ppermute | solution.py:472
  277.5 20.4 %all-to-all-start.1 = ((f32[4,256,256]{2,1,0:T(8,128)}), f32[4,256,256]{2,1,0:T(8,128)S(1)}, u32[]{:S(2)}, u32[]{:S(2)}) async-start(f32[4,256,256]{2,1,0:T(8,128)} %get-tuple-element.86), calls=%async_computation.1 | async-start | bytes 2097152 | tf_op jit(solution)/shard_map/all_to_all | solution.py:470
  298.0 19.1 %all-to-all-start.4 = ((f32[4,128,256]{2,1,0:T(8,128)}), f32[4,128,256]{2,1,0:T(8,128)S(1)}, u32[]{:S(2)}, u32[]{:S(2)}) async-start(f32[4,128,256]{2,1,0:T(8,128)} %pad_maximum_fusion.2), calls=%async_computation.6 | async-start | bytes 1048576 | tf_op jit(solution)/shard_map/all_to_all | solution.py:480
  316.2 21.3 %copy-start.23 = (f32[1,64,64]{1,2,0:T(8,128)S(1)}, f32[1,64,64]{1,2,0:T(8,128)}, u32[]{:S(2)}) copy-start(f32[1,64,64]{1,2,0:T(8,128)} %copy-done.22) | copy-start | bytes 49156
  316.2 21.3 %copy-start.18 = (f32[2,64,256]{2,1,0:T(8,128)S(1)}, f32[2,64,256]{2,1,0:T(8,128)}, u32[]{:S(2)}) copy-start(f32[2,64,256]{2,1,0:T(8,128)} %param.18) | copy-start | bytes 393220
  317.1 20.5 %copy-start.19 = (f32[2,256,64]{1,2,0:T(8,128)S(1)}, f32[2,256,64]{1,2,0:T(8,128)}, u32[]{:S(2)}) copy-start(f32[2,256,64]{1,2,0:T(8,128)} %param.19) | copy-start | bytes 393220
  317.1 20.3 %all-to-all-start.3 = ((f32[4,128,256]{2,1,0:T(8,128)}), f32[4,128,256]{2,1,0:T(8,128)S(1)}, u32[]{:S(2)}, u32[]{:S(2)}) async-start(f32[4,128,256]{2,1,0:T(8,128)} %pad_maximum_fusion.1), calls=%async_computation.4 | async-start | bytes 1048576 | tf_op jit(solution)/shard_map/all_to_all | solution.py:480
  322.4 16.8 %copy-start.17 = (f32[2,3,64,64]{3,2,1,0:T(8,128)S(1)}, f32[2,3,64,64]{3,2,1,0:T(8,128)}, u32[]{:S(2)}) copy-start(f32[2,3,64,64]{3,2,1,0:T(8,128)} %param.16) | copy-start | bytes 294916
  (22 other events, 63.9 us)
Sparse Core Ops, SparseCore 0:
  12.0 44.4 all-gather.16
  59.2 40.2 all-gather.14
  106.5 15.5 all-gather.18
  124.1 50.5 all-gather.12
  206.7 25.2 reduce-scatter.4
  243.5 24.0 reduce-scatter.2
  269.1 16.8 all-gather.22
  287.5 17.0 all-gather.20
